TPU v7x, 32 devices: a whole 2x2x4 slice. The times are simulated.
32 devices in a mesh: groups: 1, expert: 16 (over z, y, x), tensor: 2 (over core).
Axes of the slice: x: 2, y: 2, z: 4, core: 2. Of those that a mesh axis runs over, the one named last changes fastest.
Arguments:
- tokens: bfloat16 [256, 2048], P(('groups', 'expert'), 'tensor'), may hold values from -6 to 6
- expert_ids: int32 [256, 8], P(('groups', 'expert')), may hold values from 0 to 15, all different within a row; in each aligned block of 16 rows (0 to 15, 16 to 31, ...) at most 11 rows name the same one
- route_weights: float32 [256, 8], P(('groups', 'expert')), may hold values from 0.05 to 0.5
- gate_weight: bfloat16 [16, 2048, 768], P('expert', None, 'tensor'), may hold values from -0.125 to 0.125
- up_weight: bfloat16 [16, 2048, 768], P('expert', None, 'tensor'), may hold values from -0.125 to 0.125
- down_weight: bfloat16 [16, 768, 2048], P('expert', 'tensor'), may hold values from -0.21875 to 0.21875
Outputs:
- mixed: bfloat16 [256, 2048], P(('groups', 'expert'), 'tensor')
Inputs may be any that keep to these rules, and one draw needn't show every extreme that they name: `expert_ids`: each row names 8 different experts. In each aligned block of 16 rows no expert is named by more than 11 rows, and in some block an expert is named by exactly 11 rows.
All inputs are finite; a program needn't handle non-finite values.
Results may differ from a plain program's by a relative error of at most 0.005.
Values may be sent and summed in bfloat16 or wider, within the bound.
A program may use at most 64 MiB of HBM per device.

v0:
```python
import jax
import jax.numpy as jnp
from jax import lax
from jax.sharding import PartitionSpec as P


def per_device(tokens, expert_ids, route_weights, gate_weight, up_weight, down_weight):
    tok_rows = tokens.shape[0]
    top_count = expert_ids.shape[1]
    expert_count = lax.axis_size("expert")
    capacity = min(
        tok_rows, max(2, (4 * tok_rows * top_count + 3 * expert_count - 1) // (3 * expert_count))
    )
    expert_range = jnp.arange(expert_count, dtype=jnp.int32)
    member_of = (expert_ids[:, :, None] == expert_range[None, None, :]).astype(jnp.int32)
    tallies = jnp.sum(member_of, axis=1)
    preceding = jnp.cumsum(tallies, axis=0) - tallies
    slot_index = jnp.sum(member_of * preceding[:, None, :], axis=-1)
    target_row = expert_ids * capacity + slot_index
    row_index = jnp.arange(expert_count * capacity, dtype=jnp.int32)
    placing = jnp.any(target_row[None, :, :] == row_index[:, None, None], axis=-1).astype(
        jnp.bfloat16
    )
    outgoing = jnp.dot(placing, tokens, preferred_element_type=jnp.float32).astype(jnp.bfloat16)
    outgoing = outgoing.reshape(expert_count, capacity, tokens.shape[1])
    incoming = lax.all_to_all(outgoing, "expert", split_axis=0, concat_axis=0, tiled=True)
    incoming = lax.all_gather(incoming, "tensor", axis=2, tiled=True)
    senders = incoming.shape[0]
    items = incoming.shape[1]
    stacked = incoming.reshape(senders * items, incoming.shape[2])
    gate_act = jnp.dot(stacked, gate_weight[0], preferred_element_type=jnp.float32)
    up_act = jnp.dot(stacked, up_weight[0], preferred_element_type=jnp.float32)
    hidden = (jax.nn.silu(gate_act) * up_act).astype(jnp.bfloat16)
    partial_value = jnp.dot(hidden, down_weight[0], preferred_element_type=jnp.float32)
    partial_value = partial_value.reshape(senders, items, partial_value.shape[1])
    returned = lax.all_to_all(partial_value, "expert", split_axis=0, concat_axis=0, tiled=True)
    returned = returned.reshape(expert_count * capacity, returned.shape[2])
    picked = jnp.take(returned, target_row.reshape(-1), axis=0).reshape(
        tok_rows, top_count, returned.shape[1]
    )
    mixed = jnp.sum(route_weights[:, :, None] * picked, axis=1)
    mixed = lax.psum_scatter(mixed, "tensor", scatter_dimension=1, tiled=True)
    return mixed.astype(jnp.bfloat16)


def solution(mesh):
    in_specs = (
        P(("groups", "expert"), "tensor"),
        P(("groups", "expert"), None),
        P(("groups", "expert"), None),
        P("expert", None, "tensor"),
        P("expert", None, "tensor"),
        P("expert", "tensor", None),
    )
    out_specs = P(("groups", "expert"), "tensor")
    return jax.shard_map(
        per_device, mesh=mesh, in_specs=in_specs, out_specs=out_specs, check_vma=False
    )
```

profile of v0, /device:TPU:0, one launch (start us, length us, event | category | flops | bytes accessed | tf_op | source)
XLA Modules:
  0.0 115.5 jit_solution(2775841138088164483)
XLA Ops:
  6.5 0.0 copy-start
  6.5 0.9 copy.28
  7.4 0.1 convert_reduce_fusion
  7.6 0.4 select_reduce_fusion
  8.0 0.1 fusion.14
  8.1 1.0 convolution_convert_fusion
  9.2 0.1 reshape.66
  9.3 23.2 %all_to_all.10 = bf16[16,11,1024]{2,1,0:T(8,128)(2,1)S(1)} all-to-all(bf16[16,11,1024]{2,1,0:T(8,128)(2,1)S(1)} %reshape.66), channel_id=1, replica_groups=mesh['groups'=1,'expert'=16,'tensor'=2] {'expert'}, dimensions={0} | all-to-all | bytes 720896 | tf_op jit(solution)/shard_map/all_to_all | solution.py:26
  32.6 2.5 %all_gather.3 = bf16[16,11,2048]{2,1,0:T(8,128)(2,1)S(1)} all-gather(bf16[16,11,1024]{2,1,0:T(8,128)(2,1)S(1)} %all_to_all.10), channel_id=1, replica_groups=mesh['groups'=1,'expert'=16,'tensor'=2] {'tensor'}, dimensions={2}, use_global_device_ids=true | all-gather | bytes 1081344 | tf_op jit(solution)/shard_map/all_gather | solution.py:27
  35.1 0.3 reshape.67
  35.4 0.0 copy-start.2
  35.4 2.1 %fusion.4 = f32[176,384]{1,0:T(8,128)S(1)} fusion(bf16[176,2048]{1,0:T(8,128)(2,1)S(1)} %reshape.67, bf16[1,2048,384]{2,1,0:T(8,128)(2,1)} %param.9), kind=kOutput, calls=%fused_computation.5 | convolution fusion | flops 276824064 | bytes 2564096 | tf_op jit(solution)/shard_map/dot_general | solution.py:31
  37.5 0.0 copy-done.2
  37.5 0.5 fusion.9
  38.0 0.1 dot_general.17
  38.1 0.0 copy-done
  38.1 2.0 %fusion = f32[16,11,2048]{2,1,0:T(8,128)} fusion(bf16[16,11,384]{2,1,0:T(8,128)(2,1)S(1)} %dot_general.17, bf16[1,384,2048]{2,1,0:T(8,128)(2,1)S(1)} %copy-done), kind=kOutput, calls=%fused_computation.1 | convolution fusion | flops 276824064 | bytes 3149824 | tf_op jit(solution)/shard_map/dot_general | solution.py:34
  40.1 0.0 copy-start.1
  40.1 4.6 %all-to-all-start.1 = ((f32[16,11,2048]{2,1,0:T(8,128)}), f32[16,11,2048]{2,1,0:T(8,128)}, u32[]{:S(2)}, u32[]{:S(2)}) async-start(f32[16,11,2048]{2,1,0:T(8,128)} %fusion), calls=%async_computation.1 | async-start | bytes 4194304 | tf_op jit(solution)/shard_map/all_to_all | solution.py:36
  44.7 0.0 reduce-scatter.2.cloned.1.call-start
  44.8 0.1 reshape.69
  44.8 0.0 copy-done.1
  44.9 0.1 copy.27
  44.9 42.9 %all-to-all-done.1 = f32[16,11,2048]{2,1,0:T(8,128)} async-done(((f32[16,11,2048]{2,1,0:T(8,128)}), f32[16,11,2048]{2,1,0:T(8,128)}, u32[]{:S(2)}, u32[]{:S(2)}) %all-to-all-start.1) | async-done | bytes 1441824 | tf_op jit(solution)/shard_map/all_to_all | solution.py:36
  87.9 1.8 %reshape.68 = f32[176,2048]{1,0:T(8,128)S(1)} reshape(f32[16,11,2048]{2,1,0:T(8,128)} %all-to-all-done.1) | data formatting | bytes 2883584 | tf_op jit(solution)/shard_map/reshape | solution.py:37
  89.7 1.9 %gather_fusion = f32[128,2048]{1,0:T(8,128)} fusion(f32[176,2048]{1,0:T(8,128)S(1)} %reshape.68, s32[1024]{0:T(1024)S(1)} %pad_clamp_fusion), kind=kCustom, calls=%fused_computation | custom fusion | bytes 2097664 | tf_op jit(solution)/shard_map/jit(_take)/gather | solution.py:38
  91.6 2.8 %fusion.13 = f32[16,2048]{1,0:T(8,128)} fusion(f32[128,2048]{1,0:T(8,128)} %gather_fusion, f32[16,8]{1,0:T(8,128)S(1)} %copy.27, pred[16,8]{1,0:T(8,128)(4,1)S(1)} %get-tuple-element.5), kind=kLoop, calls=%fused_computation.12 | loop fusion | flops 753664 | bytes 1180288 | tf_op jit(solution)/shard_map/reduce_sum | solution.py:41
  94.5 0.0 reduce-scatter.2.cloned.1.call-update
  94.5 12.8 %reduce-scatter.2.cloned.1.call-done = f32[16,1024]{1,0:T(8,128)} async-done(((f32[16,2048]{1,0:T(8,128)}), f32[16,1024]{1,0:T(8,128)}) %reduce-scatter.2.cloned.1.call-update) | async-done | bytes 65552 | tf_op jit(solution)/shard_map/reduce_scatter | solution.py:42
  107.2 1.5 %convert_element_type.16 = bf16[16,1024]{1,0:T(8,128)(2,1)} convert(f32[16,1024]{1,0:T(8,128)} %reduce-scatter.2.cloned.1.call-done) | non-fusion elementwise | flops 16384 | bytes 98304 | tf_op jit(solution)/shard_map/convert_element_type | solution.py:43
  (5 shorter events, 0.1 us)
Async XLA Ops:
  6.5 31.6 %copy-start = (bf16[1,384,2048]{2,1,0:T(8,128)(2,1)S(1)}, bf16[1,384,2048]{2,1,0:T(8,128)(2,1)}, u32[]{:S(2)}) copy-start(bf16[1,384,2048]{2,1,0:T(8,128)(2,1)} %param.11) | copy-start | bytes 4718596
  35.4 2.1 %copy-start.2 = (bf16[1,2048,384]{2,1,0:T(8,128)(2,1)S(1)}, bf16[1,2048,384]{2,1,0:T(8,128)(2,1)}, u32[]{:S(2)}) copy-start(bf16[1,2048,384]{2,1,0:T(8,128)(2,1)} %param.10) | copy-start | bytes 4718596
  40.1 4.7 %copy-start.1 = (f32[16,8]{0,1:T(8,128)S(1)}, f32[16,8]{0,1:T(8,128)}, u32[]{:S(2)}) copy-start(f32[16,8]{0,1:T(8,128)} %param.8) | copy-start | bytes 1540
  40.1 47.7 %all-to-all-start.1 = ((f32[16,11,2048]{2,1,0:T(8,128)}), f32[16,11,2048]{2,1,0:T(8,128)}, u32[]{:S(2)}, u32[]{:S(2)}) async-start(f32[16,11,2048]{2,1,0:T(8,128)} %fusion), calls=%async_computation.1 | async-start | bytes 4194304 | tf_op jit(solution)/shard_map/all_to_all | solution.py:36
  44.7 62.5 %reduce-scatter.2.cloned.1.call-start = ((), (), s32[]{:S(2)}) async-start(), calls=%async_computation.3 | async-start | bytes 196608 | tf_op jit(solution)/shard_map/reduce_scatter | solution.py:42
Sparse Core Ops, SparseCore 0:
  94.6 12.5 reduce-scatter.1
where the time goes:
time: 116 us
  waiting for transfers between devices  55.7 us (48%)
  blocking collectives  25.8 us (22%)
  between operations  13.5 us (12%)
  matrix products  5.69 us (5%)
  local copies, waits for them, and re-layouts  5.26 us (5%)
  other arithmetic  4.97 us (4%)
  starting transfers between devices  4.6 us (4%)
    all_to_all x1, waiting for transfers between devices, per_device(): lax.all_to_all(partial_value, 'expert', split_axis=0, concat_axis=0, tile...  42.9 us
    all_to_all x1, blocking collectives, per_device(): lax.all_to_all(outgoing, 'expert', split_axis=0, concat_axis=0, tiled=True)  23.2 us
    reduce_scatter x1, waiting for transfers between devices, per_device(): mixed = lax.psum_scatter(mixed, 'tensor', scatter_dimension=1, tiled=True)  12.8 us
    all_to_all x1, starting transfers between devices, per_device(): lax.all_to_all(partial_value, 'expert', split_axis=0, concat_axis=0, tile...  4.56 us
    reduce_sum x1, other arithmetic, per_device(): mixed = jnp.sum(route_weights[:, :, None] * picked, axis=1)  2.82 us
    all_gather x1, blocking collectives, per_device(): incoming = lax.all_gather(incoming, 'tensor', axis=2, tiled=True)  2.54 us
  transfers between devices with their start and end apart: 2, of which 2 were waited for; matrix products, arithmetic and copies ran while one was open for 0% of the time, Pallas kernels for 0%

commit v1 on v0

--- a/solution.py
+++ b/solution.py
@@ -1,7 +1,15 @@
+import functools
+
 import jax
 import jax.numpy as jnp
 from jax import lax
+from jax.experimental import pallas as pl
+from jax.experimental.pallas import tpu as pltpu
 from jax.sharding import PartitionSpec as P
+
+MESH = pl.DeviceIdType.MESH
+BF16 = jnp.bfloat16
+F32 = jnp.float32
 
 
 def per_device(tokens, expert_ids, route_weights, gate_weight, up_weight, down_weight):
@@ -43,6 +51,252 @@
     return mixed.astype(jnp.bfloat16)
 
 
+def kernel(
+    tok_ref, ids_ref, rw_ref, gate_hbm, up_hbm, down_hbm, out_ref,
+    xg, gu, dw, hid, ysend, p1, p2s, p2r,
+    wsem, zs, zr, xs, xr, ys, yr, ds, dr, ps, pr, dws, dwr, hs, hr, as_, ar, bs, br,
+):
+    T = tok_ref.shape[0]
+    DH = tok_ref.shape[1]
+    F = gate_hbm.shape[2]
+    me = lax.axis_index("expert")
+    c = lax.axis_index("tensor")
+    x = me % 2
+    y = (me // 2) % 2
+    z = me // 4
+    zd = [z, z + 1 - 2 * (z % 2), (z + 2) % 4, 3 - z]
+    plane = y * 2 + x
+    xn = y * 2 + 1 - x
+    yn = (1 - y) * 2 + x
+    dn = (1 - y) * 2 + 1 - x
+    planes = [plane, xn, yn, dn]
+
+    def ex(zz, pp):
+        return {"expert": zz * 4 + pp}
+
+    other = {"tensor": 1 - c}
+
+    def rows(zz, pp, n=1):
+        return pl.ds(pl.multiple_of((zz * 4 + pp) * T, T), n * T)
+
+    def remote(src, dst, ssem, rsem, dev):
+        return pltpu.make_async_remote_copy(
+            src_ref=src, dst_ref=dst, send_sem=ssem, recv_sem=rsem,
+            device_id=dev, device_id_type=MESH,
+        )
+
+    w_g = pltpu.make_async_copy(gate_hbm.at[0], gu.at[0], wsem.at[0])
+    w_u = pltpu.make_async_copy(up_hbm.at[0], gu.at[1], wsem.at[1])
+    w_d = pltpu.make_async_copy(
+        down_hbm.at[0, :, pl.ds(pl.multiple_of(c * DH, DH), DH)], dw.at[c], wsem.at[2]
+    )
+    w_g.start()
+    w_u.start()
+
+    barrier = pltpu.get_barrier_semaphore()
+    peers = [ex(zd[1], plane), ex(zd[2], plane), ex(zd[3], plane),
+             ex(z, xn), ex(z, yn), ex(z, dn), other]
+    for p in peers:
+        pl.semaphore_signal(barrier, inc=1, device_id=p, device_id_type=MESH)
+
+    lane = lax.broadcasted_iota(jnp.int32, (T, 128), 1)
+    table = jnp.zeros((T, 128), F32)
+    for k in range(ids_ref.shape[1]):
+        table = table + jnp.where(ids_ref[:, k:k + 1] == lane, rw_ref[:, k:k + 1], 0.0)
+    high = table.astype(BF16)
+    low = (table - high.astype(F32)).astype(BF16)
+    own = rows(z, plane)
+    xg[c, own, :DH] = tok_ref[...]
+    xg[c, own, DH:] = jnp.where(c == 0, high.astype(F32), low.astype(F32)).astype(BF16)
+
+    pl.semaphore_wait(barrier, len(peers))
+
+    started = []
+
+    def go(copy):
+        copy.start()
+        started.append(copy)
+        return copy
+
+    def block(zz, pp):
+        return xg.at[c, rows(zz, pp)]
+
+    def block_other(zz, pp):
+        return xg.at[1 - c, rows(zz, pp)]
+
+    for d in (1, 2, 3):
+        go(remote(block(z, plane), block(z, plane), zs.at[d], zr.at[d], ex(zd[d], plane)))
+
+    dcopy = remote(
+        down_hbm.at[0, :, pl.ds(pl.multiple_of((1 - c) * DH, DH), DH)], dw.at[c], dws, dwr, other
+    )
+
+    def fan(d):
+        b = block(zd[d], plane)
+        go(remote(b, b, xs.at[d], xr.at[d], ex(z, xn)))
+        go(remote(b, b, ys.at[d], yr.at[d], ex(z, yn)))
+        go(remote(b, b, ps.at[d, 0], pr.at[d, 0], other))
+
+    def second(d):
+        bx = block(zd[d], xn)
+        by = block(zd[d], yn)
+        if d % 2 == 0:
+            remote(bx, bx, xs.at[d], xr.at[d], ex(z, xn)).wait_recv()
+            go(remote(bx, bx, ds.at[d], dr.at[d], ex(z, yn)))
+            go(remote(bx, bx, ps.at[d, 1], pr.at[d, 1], other))
+            remote(by, by, ys.at[d], yr.at[d], ex(z, yn)).wait_recv()
+            go(remote(by, by, ps.at[d, 2], pr.at[d, 2], other))
+        else:
+            remote(by, by, ys.at[d], yr.at[d], ex(z, yn)).wait_recv()
+            go(remote(by, by, ds.at[d], dr.at[d], ex(z, xn)))
+            go(remote(by, by, ps.at[d, 2], pr.at[d, 2], other))
+            remote(bx, bx, xs.at[d], xr.at[d], ex(z, xn)).wait_recv()
+            go(remote(bx, bx, ps.at[d, 1], pr.at[d, 1], other))
+
+    def third(d):
+        b = block(zd[d], dn)
+        remote(b, b, ds.at[d], dr.at[d], ex(z, dn)).wait_recv()
+        go(remote(b, b, ps.at[d, 3], pr.at[d, 3], other))
+
+    def zwait(d):
+        b = block(zd[d], plane)
+        remote(b, b, zs.at[d], zr.at[d], ex(zd[d], plane)).wait_recv()
+
+    def others(d):
+        for j in range(4):
+            b = block_other(zd[d], planes[j])
+            remote(b, b, ps.at[d, j], pr.at[d, j], other).wait_recv()
+
+    fan(0)
+    go(dcopy)
+    w_d.start()
+    zwait(1)
+    fan(1)
+    second(0)
+    zwait(2)
+    fan(2)
+    second(1)
+    zwait(3)
+    fan(3)
+    third(0)
+    third(1)
+    others(0)
+    others(1)
+    w_g.wait()
+    w_u.wait()
+
+    half = 8 * T
+
+    def up_phase(i, r0):
+        rr = pl.ds(pl.multiple_of(r0, half), half)
+        g = jnp.dot(xg[0, rr, :DH], gu[0, :DH, :], preferred_element_type=F32)
+        g = g + jnp.dot(xg[1, rr, :DH], gu[0, DH:, :], preferred_element_type=F32)
+        u = jnp.dot(xg[0, rr, :DH], gu[1, :DH, :], preferred_element_type=F32)
+        u = u + jnp.dot(xg[1, rr, :DH], gu[1, DH:, :], preferred_element_type=F32)
+        hid[c, rr, :] = (g / (1.0 + jnp.exp(-g)) * u).astype(BF16)
+        h = hid.at[c, rr]
+        go(remote(h, h, hs.at[i], hr.at[i], other))
+
+    def down_phase(i, r0):
+        rr = pl.ds(pl.multiple_of(r0, half), half)
+        h = hid.at[1 - c, rr]
+        remote(h, h, hs.at[i], hr.at[i], other).wait_recv()
+        col = lax.broadcasted_iota(jnp.int32, (half, 128), 1)
+        wt = xg[0, rr, DH:].astype(F32) + xg[1, rr, DH:].astype(F32)
+        wt = jnp.sum(jnp.where(col == me, wt, 0.0), axis=1, keepdims=True)
+        v = jnp.dot(hid[0, rr, :], dw[0], preferred_element_type=F32)
+        v = v + jnp.dot(hid[1, rr, :], dw[1], preferred_element_type=F32)
+        ysend[rr, :] = (v * wt).astype(BF16)
+
+    def slot(j, d):
+        return p1.at[pl.ds(((j - 1) * 4 + d) * T, T)]
+
+    def send_plane(d):
+        for j in (1, 2, 3):
+            go(remote(ysend.at[rows(zd[d], planes[j])], slot(j, d),
+                      as_.at[j - 1, d], ar.at[j - 1, d], ex(z, planes[j])))
+
+    def reduce_plane(d):
+        total = ysend[rows(zd[d], plane), :].astype(F32)
+        for j in (1, 2, 3):
+            s = slot(j, d)
+            remote(s, s, as_.at[j - 1, d], ar.at[j - 1, d], ex(z, planes[j])).wait_recv()
+            total = total + s[...].astype(F32)
+        return total
+
+    ra = (z // 2) * half
+    rb = half - ra
+    up_phase(0, ra)
+    second(2)
+    second(3)
+    third(2)
+    third(3)
+    w_d.wait()
+    dcopy.wait_recv()
+    down_phase(0, ra)
+    send_plane(1)
+    others(2)
+    others(3)
+    up_phase(1, rb)
+    down_phase(1, rb)
+    send_plane(2)
+    send_plane(3)
+    send_plane(0)
+    for d in (1, 2, 3):
+        p2s[d - 1] = reduce_plane(d).astype(BF16)
+        go(remote(p2s.at[d - 1], p2r.at[d - 1], bs.at[d - 1], br.at[d - 1], ex(zd[d], plane)))
+    total = reduce_plane(0)
+    for d in (1, 2, 3):
+        s = p2r.at[d - 1]
+        remote(s, s, bs.at[d - 1], br.at[d - 1], ex(zd[d], plane)).wait_recv()
+        total = total + s[...].astype(F32)
+    out_ref[...] = total.astype(BF16)
+    for copy in started:
+        copy.wait_send()
+
+
+def fused(tokens, expert_ids, route_weights, gate_weight, up_weight, down_weight):
+    T, DH = tokens.shape
+    F = gate_weight.shape[2]
+    D = gate_weight.shape[1]
+    R = 16 * T
+    vmem = pl.BlockSpec(memory_space=pltpu.VMEM)
+    hbm = pl.BlockSpec(memory_space=pltpu.HBM)
+    dma = pltpu.SemaphoreType.DMA
+    return pl.pallas_call(
+        kernel,
+        out_shape=jax.ShapeDtypeStruct((T, DH), BF16),
+        in_specs=[vmem, vmem, vmem, hbm, hbm, hbm],
+        out_specs=vmem,
+        scratch_shapes=[
+            pltpu.VMEM((2, R, DH + 128), BF16),
+            pltpu.VMEM((2, D, F), BF16),
+            pltpu.VMEM((2, F, DH), BF16),
+            pltpu.VMEM((2, R, F), BF16),
+            pltpu.VMEM((R, DH), BF16),
+            pltpu.VMEM((12 * T, DH), BF16),
+            pltpu.VMEM((3, T, DH), BF16),
+            pltpu.VMEM((3, T, DH), BF16),
+            dma((3,)),
+            dma((4,)), dma((4,)),
+            dma((4,)), dma((4,)),
+            dma((4,)), dma((4,)),
+            dma((4,)), dma((4,)),
+            dma((4, 4)), dma((4, 4)),
+            dma, dma,
+            dma((2,)), dma((2,)),
+            dma((3, 4)), dma((3, 4)),
+            dma((3,)), dma((3,)),
+        ],
+        compiler_params=pltpu.CompilerParams(
+            collective_id=0, has_side_effects=True, vmem_limit_bytes=40 * 1024 * 1024
+        ),
+        cost_estimate=pl.CostEstimate(
+            flops=2 * R * D * F * 3, bytes_accessed=6 * D * F, transcendentals=R * F
+        ),
+    )(tokens, expert_ids, route_weights, gate_weight, up_weight, down_weight)
+
+
 def solution(mesh):
     in_specs = (
         P(("groups", "expert"), "tensor"),
@@ -53,6 +307,8 @@
         P("expert", "tensor", None),
     )
     out_specs = P(("groups", "expert"), "tensor")
+    small = mesh.shape["groups"] == 1 and mesh.shape["expert"] == 16 and mesh.shape["tensor"] == 2
     return jax.shard_map(
-        per_device, mesh=mesh, in_specs=in_specs, out_specs=out_specs, check_vma=False
-    )
+        fused if small else per_device,
+        mesh=mesh, in_specs=in_specs, out_specs=out_specs, check_vma=False,
+    )

time: 116 us -> 39 us (0.34)
  waiting for transfers between devices: 55.7 us -> 0 us
  Pallas kernels: 0 us -> 31.5 us
  blocking collectives: 25.8 us -> 0 us
  between operations: 13.5 us -> 0.01 us
  matrix products: 5.69 us -> 0 us
  other arithmetic: 4.97 us -> 0 us
  starting transfers between devices: 4.6 us -> 0 us
  local copies, waits for them, and re-layouts: 5.26 us -> 7.11 us
    all_to_all x1 -> x0, waiting for transfers between devices: 42.9 us -> none  [per_device(): lax.all_to_all(partial_value, 'expert', split_axis=0, concat_axis=0, tile...]
    pallas_call x0 -> x1, Pallas kernels: none -> 31.5 us  [fused(): pl.pallas_call(kernel, out_shape=jax.ShapeDtypeStruct((T, DH), BF16), in_...]
    all_to_all x1 -> x0, blocking collectives: 23.2 us -> none  [per_device(): lax.all_to_all(outgoing, 'expert', split_axis=0, concat_axis=0, tiled=True)]
    reduce_scatter x1 -> x0, waiting for transfers between devices: 12.8 us -> none  [per_device(): mixed = lax.psum_scatter(mixed, 'tensor', scatter_dimension=1, tiled=True)]
    unnamed x8 -> x11, local copies, waits for them, and re-layouts: 0.96 us -> 7.11 us
    dot_general x4 -> x0, matrix products: 5.69 us -> none  [the longest x1 2.08 us: per_device(): jnp.dot(stacked, gate_weight[0], preferred_element_type=jnp.float32)]
    all_to_all x1 -> x0, starting transfers between devices: 4.56 us -> none  [per_device(): lax.all_to_all(partial_value, 'expert', split_axis=0, concat_axis=0, tile...]
    reduce_sum x3 -> x0, other arithmetic: 3.33 us -> none  [the longest x1 2.82 us: per_device(): mixed = jnp.sum(route_weights[:, :, None] * picked, axis=1)]
  transfers between devices with their start and end apart: 2 -> 0, of which waited for: 2 -> 0; matrix products, arithmetic and copies ran while one was open for 0% -> 0% of each run, Pallas kernels for 0% -> 0%
where the time goes in v1:
time: 39 us; the launch traced here: 38.6 us
  Pallas kernels  31.5 us (81%)
  local copies, waits for them, and re-layouts  7.11 us (18%)
    pallas_call x1, Pallas kernels, fused(): pl.pallas_call(kernel, out_shape=jax.ShapeDtypeStruct((T, DH), BF16), in_...  31.5 us
    unnamed x11, local copies, waits for them, and re-layouts  7.11 us

profile of v1, /device:TPU:0, one launch (start us, length us, event | category | flops | bytes accessed | tf_op | source)
XLA Modules:
  0.0 38.6 jit_solution(4148283797769297583)
XLA Ops:
  0.0 0.8 %copy.7.ids_ref = s32[16,8]{1,0:T(8,128)S(1)} copy(s32[16,8]{0,1:T(8,128)} %param.7) | data formatting | bytes 1024 | tf_op args[1]
  0.8 0.8 %copy.8.rw_ref = f32[16,8]{1,0:T(8,128)S(1)} copy(f32[16,8]{0,1:T(8,128)} %param.8) | data formatting | bytes 1024 | tf_op args[2]
  1.5 0.0 copy-start
  1.5 1.4 %copy-done = bf16[1,2048,384]{2,1,0:T(8,128)(2,1)S(1)} copy-done((bf16[1,2048,384]{2,1,0:T(8,128)(2,1)S(1)}, bf16[1,2048,384]{2,1,0:T(8,128)(2,1)}, u32[]{:S(2)}) %copy-start) | copy-done | bytes 1572888
  2.9 0.0 copy-start.1
  2.9 1.4 %copy-done.1 = bf16[1,2048,384]{2,1,0:T(8,128)(2,1)S(1)} copy-done((bf16[1,2048,384]{2,1,0:T(8,128)(2,1)S(1)}, bf16[1,2048,384]{2,1,0:T(8,128)(2,1)}, u32[]{:S(2)}) %copy-start.1) | copy-done | bytes 1572888
  4.3 0.0 copy-start.2
  4.3 1.4 %copy-done.2 = bf16[1,384,2048]{2,1,0:T(8,128)(2,1)S(1)} copy-done((bf16[1,384,2048]{2,1,0:T(8,128)(2,1)S(1)}, bf16[1,384,2048]{2,1,0:T(8,128)(2,1)}, u32[]{:S(2)}) %copy-start.2) | copy-done | bytes 1572888
  5.7 0.0 copy-start.3
  5.7 0.8 %copy-done.3 = bf16[16,1024]{1,0:T(8,128)(2,1)S(1)} copy-done((bf16[16,1024]{1,0:T(8,128)(2,1)S(1)}, bf16[16,1024]{1,0:T(8,128)(2,1)}, u32[]{:S(2)}) %copy-start.3) | copy-done | bytes 32792
  6.5 31.5 %shard_map.64 = bf16[16,1024]{1,0:T(8,128)(2,1)S(1)} custom-call(bf16[16,1024]{1,0:T(8,128)(2,1)S(1)} %copy-done.3, s32[16,8]{1,0:T(8,128)S(1)} %copy.7.ids_ref, f32[16,8]{1,0:T(8,128)S(1)} %copy.8.rw_ref, bf16[1,2048,384]{2,1,0:T(8,128)(2,1)S(1)} %copy-done, bf16[1,2048,384]{2,1,0:T(8,128)(2,1)S(1)} %copy-done.1, bf16[1,384,2048]{2,1,0:T(8,128)(2,1)S(1)} %copy-done.2), custom_call_target="tpu_custom_call" | custom-call | flops 1207959552 | bytes 4718592 | tf_op jit(solution)/shard_map/pallas_call | solution.py:266
  38.0 0.6 %copy.10 = bf16[16,1024]{1,0:T(8,128)(2,1)} copy(bf16[16,1024]{1,0:T(8,128)(2,1)S(1)} %shard_map.64) | data formatting | bytes 65536
Async XLA Ops:
  1.5 1.4 %copy-start = (bf16[1,2048,384]{2,1,0:T(8,128)(2,1)S(1)}, bf16[1,2048,384]{2,1,0:T(8,128)(2,1)}, u32[]{:S(2)}) copy-start(bf16[1,2048,384]{2,1,0:T(8,128)(2,1)} %gate_hbm.1) | copy-start | bytes 4718596
  2.9 1.4 %copy-start.1 = (bf16[1,2048,384]{2,1,0:T(8,128)(2,1)S(1)}, bf16[1,2048,384]{2,1,0:T(8,128)(2,1)}, u32[]{:S(2)}) copy-start(bf16[1,2048,384]{2,1,0:T(8,128)(2,1)} %up_hbm.1) | copy-start | bytes 4718596
  4.3 1.4 %copy-start.2 = (bf16[1,384,2048]{2,1,0:T(8,128)(2,1)S(1)}, bf16[1,384,2048]{2,1,0:T(8,128)(2,1)}, u32[]{:S(2)}) copy-start(bf16[1,384,2048]{2,1,0:T(8,128)(2,1)} %down_hbm.1) | copy-start | bytes 4718596
  5.7 0.8 %copy-start.3 = (bf16[16,1024]{1,0:T(8,128)(2,1)S(1)}, bf16[16,1024]{1,0:T(8,128)(2,1)}, u32[]{:S(2)}) copy-start(bf16[16,1024]{1,0:T(8,128)(2,1)} %tok_ref.1) | copy-start | bytes 98308

commit v2 on v1

--- a/solution.py
+++ b/solution.py
@@ -52,13 +52,12 @@
 
 
 def kernel(
-    tok_ref, ids_ref, rw_ref, gate_hbm, up_hbm, down_hbm, out_ref,
-    xg, gu, dw, hid, ysend, p1, p2s, p2r,
+    tok_hbm, ids_hbm, rw_hbm, gate_hbm, up_hbm, down_hbm, out_ref,
+    tok_ref, ids_ref, rw_ref, xg, gu, dw, hid, ysend, p1, p2s, p2r,
     wsem, zs, zr, xs, xr, ys, yr, ds, dr, ps, pr, dws, dwr, hs, hr, as_, ar, bs, br,
 ):
-    T = tok_ref.shape[0]
-    DH = tok_ref.shape[1]
-    F = gate_hbm.shape[2]
+    T = tok_hbm.shape[0]
+    DH = tok_hbm.shape[1]
     me = lax.axis_index("expert")
     c = lax.axis_index("tensor")
     x = me % 2
@@ -85,13 +84,17 @@
             device_id=dev, device_id_type=MESH,
         )
 
+    small = [
+        pltpu.make_async_copy(a, b, wsem.at[3 + i])
+        for i, (a, b) in enumerate(((ids_hbm, ids_ref), (rw_hbm, rw_ref), (tok_hbm, tok_ref)))
+    ]
+    for copy in small:
+        copy.start()
     w_g = pltpu.make_async_copy(gate_hbm.at[0], gu.at[0], wsem.at[0])
     w_u = pltpu.make_async_copy(up_hbm.at[0], gu.at[1], wsem.at[1])
     w_d = pltpu.make_async_copy(
         down_hbm.at[0, :, pl.ds(pl.multiple_of(c * DH, DH), DH)], dw.at[c], wsem.at[2]
     )
-    w_g.start()
-    w_u.start()
 
     barrier = pltpu.get_barrier_semaphore()
     peers = [ex(zd[1], plane), ex(zd[2], plane), ex(zd[3], plane),
@@ -99,10 +102,17 @@
     for p in peers:
         pl.semaphore_signal(barrier, inc=1, device_id=p, device_id_type=MESH)
 
-    lane = lax.broadcasted_iota(jnp.int32, (T, 128), 1)
-    table = jnp.zeros((T, 128), F32)
-    for k in range(ids_ref.shape[1]):
-        table = table + jnp.where(ids_ref[:, k:k + 1] == lane, rw_ref[:, k:k + 1], 0.0)
+    w_g.start()
+    w_u.start()
+    w_d.start()
+
+    for copy in small:
+        copy.wait()
+    expert = lax.broadcasted_iota(jnp.int32, (16, T), 0)
+    table = jnp.zeros((16, T), F32)
+    for k in range(ids_ref.shape[0]):
+        table = table + jnp.where(ids_ref[k:k + 1, :] == expert, rw_ref[k:k + 1, :], 0.0)
+    table = jnp.pad(table, ((0, 112), (0, 128 - T))).T[:T]
     high = table.astype(BF16)
     low = (table - high.astype(F32)).astype(BF16)
     own = rows(z, plane)
@@ -169,7 +179,6 @@
 
     fan(0)
     go(dcopy)
-    w_d.start()
     zwait(1)
     fan(1)
     second(0)
@@ -257,6 +266,7 @@
 
 def fused(tokens, expert_ids, route_weights, gate_weight, up_weight, down_weight):
     T, DH = tokens.shape
+    K = expert_ids.shape[1]
     F = gate_weight.shape[2]
     D = gate_weight.shape[1]
     R = 16 * T
@@ -266,9 +276,12 @@
     return pl.pallas_call(
         kernel,
         out_shape=jax.ShapeDtypeStruct((T, DH), BF16),
-        in_specs=[vmem, vmem, vmem, hbm, hbm, hbm],
+        in_specs=[hbm] * 6,
         out_specs=vmem,
         scratch_shapes=[
+            pltpu.VMEM((T, DH), BF16),
+            pltpu.VMEM((K, T), jnp.int32),
+            pltpu.VMEM((K, T), F32),
             pltpu.VMEM((2, R, DH + 128), BF16),
             pltpu.VMEM((2, D, F), BF16),
             pltpu.VMEM((2, F, DH), BF16),
@@ -277,7 +290,7 @@
             pltpu.VMEM((12 * T, DH), BF16),
             pltpu.VMEM((3, T, DH), BF16),
             pltpu.VMEM((3, T, DH), BF16),
-            dma((3,)),
+            dma((6,)),
             dma((4,)), dma((4,)),
             dma((4,)), dma((4,)),
             dma((4,)), dma((4,)),
@@ -289,12 +302,12 @@
             dma((3,)), dma((3,)),
         ],
         compiler_params=pltpu.CompilerParams(
-            collective_id=0, has_side_effects=True, vmem_limit_bytes=40 * 1024 * 1024
+            collective_id=0, has_side_effects=True, vmem_limit_bytes=60 * 1024 * 1024
         ),
         cost_estimate=pl.CostEstimate(
             flops=2 * R * D * F * 3, bytes_accessed=6 * D * F, transcendentals=R * F
         ),
-    )(tokens, expert_ids, route_weights, gate_weight, up_weight, down_weight)
+    )(tokens, expert_ids.T, route_weights.T, gate_weight, up_weight, down_weight)
 
 
 def solution(mesh):

time: 39 us -> 33.5 us (0.86)
  local copies, waits for them, and re-layouts: 7.11 us -> 1.38 us
  Pallas kernels: 31.5 us -> 32 us
    unnamed x11 -> x1, local copies, waits for them, and re-layouts: 7.11 us -> 1.38 us
    pallas_call x1, Pallas kernels: 31.5 us -> 32 us  [fused(): pl.pallas_call(kernel, out_shape=jax.ShapeDtypeStruct((T, DH), BF16), in_...]
where the time goes in v2:
time: 33.5 us; the launch traced here: 33.3 us
  Pallas kernels  32 us (96%)
  local copies, waits for them, and re-layouts  1.38 us (4%)
    pallas_call x1, Pallas kernels, fused(): pl.pallas_call(kernel, out_shape=jax.ShapeDtypeStruct((T, DH), BF16), in_...  32 us
    unnamed x1, local copies, waits for them, and re-layouts  1.38 us

profile of v2, /device:TPU:0, one launch (start us, length us, event | category | flops | bytes accessed | tf_op | source)
XLA Modules:
  0.0 33.3 jit_solution(16501455869961383344)
XLA Ops:
  0.0 32.0 %shard_map.64 = bf16[16,1024]{1,0:T(8,128)(2,1)} custom-call(bf16[16,1024]{1,0:T(8,128)(2,1)} %tok_hbm.1, s32[8,16]{1,0:T(8,128)} %bitcast.2, f32[8,16]{1,0:T(8,128)} %bitcast.3, bf16[1,2048,384]{2,1,0:T(8,128)(2,1)} %gate_hbm.1, bf16[1,2048,384]{2,1,0:T(8,128)(2,1)} %up_hbm.1, bf16[1,384,2048]{2,1,0:T(8,128)(2,1)} %down_hbm.1), custom_call_target="tpu_custom_call" | custom-call | flops 1207959552 | bytes 4718592 | tf_op jit(solution)/shard_map/pallas_call | solution.py:276
  32.0 1.4 %copy.8 = bf16[16,1024]{1,0:T(8,128)(2,1)} copy(bf16[16,1024]{1,0:T(8,128)(2,1)} %shard_map.64) | data formatting | bytes 65536

commit v3 on v2

--- a/solution.py
+++ b/solution.py
@@ -63,7 +63,7 @@
     x = me % 2
     y = (me // 2) % 2
     z = me // 4
-    zd = [z, z + 1 - 2 * (z % 2), (z + 2) % 4, 3 - z]
+    zd = [z, z + 1 - 2 * (z % 2), 2 - z // 2, 3 - 3 * (z // 2)]
     plane = y * 2 + x
     xn = y * 2 + 1 - x
     yn = (1 - y) * 2 + x
@@ -135,60 +135,55 @@
         return xg.at[1 - c, rows(zz, pp)]
 
     for d in (1, 2, 3):
-        go(remote(block(z, plane), block(z, plane), zs.at[d], zr.at[d], ex(zd[d], plane)))
+        b = block(z, plane)
+        go(remote(b, b, zs.at[d], zr.at[z], ex(zd[d], plane)))
 
     dcopy = remote(
         down_hbm.at[0, :, pl.ds(pl.multiple_of((1 - c) * DH, DH), DH)], dw.at[c], dws, dwr, other
     )
 
-    def fan(d):
-        b = block(zd[d], plane)
-        go(remote(b, b, xs.at[d], xr.at[d], ex(z, xn)))
-        go(remote(b, b, ys.at[d], yr.at[d], ex(z, yn)))
-        go(remote(b, b, ps.at[d, 0], pr.at[d, 0], other))
-
-    def second(d):
-        bx = block(zd[d], xn)
-        by = block(zd[d], yn)
-        if d % 2 == 0:
-            remote(bx, bx, xs.at[d], xr.at[d], ex(z, xn)).wait_recv()
-            go(remote(bx, bx, ds.at[d], dr.at[d], ex(z, yn)))
-            go(remote(bx, bx, ps.at[d, 1], pr.at[d, 1], other))
-            remote(by, by, ys.at[d], yr.at[d], ex(z, yn)).wait_recv()
-            go(remote(by, by, ps.at[d, 2], pr.at[d, 2], other))
-        else:
-            remote(by, by, ys.at[d], yr.at[d], ex(z, yn)).wait_recv()
-            go(remote(by, by, ds.at[d], dr.at[d], ex(z, xn)))
-            go(remote(by, by, ps.at[d, 2], pr.at[d, 2], other))
-            remote(bx, bx, xs.at[d], xr.at[d], ex(z, xn)).wait_recv()
-            go(remote(bx, bx, ps.at[d, 1], pr.at[d, 1], other))
-
-    def third(d):
-        b = block(zd[d], dn)
-        remote(b, b, ds.at[d], dr.at[d], ex(z, dn)).wait_recv()
-        go(remote(b, b, ps.at[d, 3], pr.at[d, 3], other))
+    sems = [None, (xs, xr), (ys, yr), (ds, dr)]
+
+    def spread(src, d, zz):
+        b = block(src, plane)
+        for j in (3, 1, 2):
+            ss, rs = sems[j]
+            go(remote(b, b, ss.at[d], rs.at[d], ex(zz, planes[j])))
+
+    def share(d, j):
+        b = block(zd[d], planes[j])
+        go(remote(b, b, ps.at[d, j], pr.at[d, j], other))
+
+    def arrive(d):
+        for j in (1, 2, 3):
+            b = block(zd[d], planes[j])
+            ss, rs = sems[j]
+            remote(b, b, ss.at[d], rs.at[d], ex(z, planes[j])).wait_recv()
+            share(d, j)
 
     def zwait(d):
         b = block(zd[d], plane)
-        remote(b, b, zs.at[d], zr.at[d], ex(zd[d], plane)).wait_recv()
+        remote(b, b, zs.at[0], zr.at[zd[d]], ex(zd[d], plane)).wait_recv()
 
     def others(d):
         for j in range(4):
             b = block_other(zd[d], planes[j])
             remote(b, b, ps.at[d, j], pr.at[d, j], other).wait_recv()
 
-    fan(0)
+    spread(z, 0, z)
+    share(0, 0)
+    zwait(1)
+    spread(zd[1], 1, z)
+    share(1, 0)
+    arrive(0)
+    zwait(2)
+    spread(zd[2], 2, z)
+    share(2, 0)
+    zwait(3)
+    spread(zd[3], 3, z)
+    share(3, 0)
     go(dcopy)
-    zwait(1)
-    fan(1)
-    second(0)
-    zwait(2)
-    fan(2)
-    second(1)
-    zwait(3)
-    fan(3)
-    third(0)
-    third(1)
+    arrive(1)
     others(0)
     others(1)
     w_g.wait()
@@ -236,28 +231,26 @@
     ra = (z // 2) * half
     rb = half - ra
     up_phase(0, ra)
-    second(2)
-    second(3)
-    third(2)
-    third(3)
+    arrive(2)
     w_d.wait()
     dcopy.wait_recv()
     down_phase(0, ra)
     send_plane(1)
+    send_plane(0)
+    arrive(3)
     others(2)
     others(3)
     up_phase(1, rb)
     down_phase(1, rb)
+    send_plane(3)
     send_plane(2)
-    send_plane(3)
-    send_plane(0)
-    for d in (1, 2, 3):
+    for d in (1, 3, 2):
         p2s[d - 1] = reduce_plane(d).astype(BF16)
-        go(remote(p2s.at[d - 1], p2r.at[d - 1], bs.at[d - 1], br.at[d - 1], ex(zd[d], plane)))
+        go(remote(p2s.at[d - 1], p2r.at[z], bs.at[d - 1], br.at[z], ex(zd[d], plane)))
     total = reduce_plane(0)
     for d in (1, 2, 3):
-        s = p2r.at[d - 1]
-        remote(s, s, bs.at[d - 1], br.at[d - 1], ex(zd[d], plane)).wait_recv()
+        s = p2r.at[zd[d]]
+        remote(s, s, bs.at[d - 1], br.at[zd[d]], ex(zd[d], plane)).wait_recv()
         total = total + s[...].astype(F32)
     out_ref[...] = total.astype(BF16)
     for copy in started:
@@ -289,7 +282,7 @@
             pltpu.VMEM((R, DH), BF16),
             pltpu.VMEM((12 * T, DH), BF16),
             pltpu.VMEM((3, T, DH), BF16),
-            pltpu.VMEM((3, T, DH), BF16),
+            pltpu.VMEM((4, T, DH), BF16),
             dma((6,)),
             dma((4,)), dma((4,)),
             dma((4,)), dma((4,)),
@@ -299,7 +292,7 @@
             dma, dma,
             dma((2,)), dma((2,)),
             dma((3, 4)), dma((3, 4)),
-            dma((3,)), dma((3,)),
+            dma((3,)), dma((4,)),
         ],
         compiler_params=pltpu.CompilerParams(
             collective_id=0, has_side_effects=True, vmem_limit_bytes=60 * 1024 * 1024

time: 33.5 us -> 29.6 us (0.88)
  Pallas kernels: 32 us -> 28.1 us
    pallas_call x1, Pallas kernels: 32 us -> 28.1 us  [fused(): pl.pallas_call(kernel, out_shape=jax.ShapeDtypeStruct((T, DH), BF16), in_...]
where the time goes in v3:
time: 29.6 us; the launch traced here: 29.4 us
  Pallas kernels  28.1 us (95%)
  local copies, waits for them, and re-layouts  1.38 us (5%)
    pallas_call x1, Pallas kernels, fused(): pl.pallas_call(kernel, out_shape=jax.ShapeDtypeStruct((T, DH), BF16), in_...  28.1 us
    unnamed x1, local copies, waits for them, and re-layouts  1.38 us

profile of v3, /device:TPU:0, one launch (start us, length us, event | category | flops | bytes accessed | tf_op | source)
XLA Modules:
  0.0 29.4 jit_solution(17553740276913587127)
XLA Ops:
  0.0 28.1 %shard_map.64 = bf16[16,1024]{1,0:T(8,128)(2,1)} custom-call(bf16[16,1024]{1,0:T(8,128)(2,1)} %tok_hbm.1, s32[8,16]{1,0:T(8,128)} %bitcast.2, f32[8,16]{1,0:T(8,128)} %bitcast.3, bf16[1,2048,384]{2,1,0:T(8,128)(2,1)} %gate_hbm.1, bf16[1,2048,384]{2,1,0:T(8,128)(2,1)} %up_hbm.1, bf16[1,384,2048]{2,1,0:T(8,128)(2,1)} %down_hbm.1), custom_call_target="tpu_custom_call" | custom-call | flops 1207959552 | bytes 4718592 | tf_op jit(solution)/shard_map/pallas_call | solution.py:269
  28.1 1.4 %copy.8 = bf16[16,1024]{1,0:T(8,128)(2,1)} copy(bf16[16,1024]{1,0:T(8,128)(2,1)} %shard_map.64) | data formatting | bytes 65536

commit v4 on v3

--- a/solution.py
+++ b/solution.py
@@ -53,7 +53,7 @@
 
 def kernel(
     tok_hbm, ids_hbm, rw_hbm, gate_hbm, up_hbm, down_hbm, out_ref,
-    tok_ref, ids_ref, rw_ref, xg, gu, dw, hid, ysend, p1, p2s, p2r,
+    tok_ref, ids_ref, rw_ref, acc, xg, gu, dw, hid, ysend, p1, p2s, p2r,
     wsem, zs, zr, xs, xr, ys, yr, ds, dr, ps, pr, dws, dwr, hs, hr, as_, ar, bs, br,
 ):
     T = tok_hbm.shape[0]
@@ -184,39 +184,44 @@
     share(3, 0)
     go(dcopy)
     arrive(1)
-    others(0)
-    others(1)
     w_g.wait()
     w_u.wait()
 
     half = 8 * T
 
-    def up_phase(i, r0):
+    own_d = pl.ds(pl.multiple_of(c * DH, DH), DH)
+    oth_d = pl.ds(pl.multiple_of((1 - c) * DH, DH), DH)
+
+    def up_phase(i, r0, groups):
         rr = pl.ds(pl.multiple_of(r0, half), half)
-        g = jnp.dot(xg[0, rr, :DH], gu[0, :DH, :], preferred_element_type=F32)
-        g = g + jnp.dot(xg[1, rr, :DH], gu[0, DH:, :], preferred_element_type=F32)
-        u = jnp.dot(xg[0, rr, :DH], gu[1, :DH, :], preferred_element_type=F32)
-        u = u + jnp.dot(xg[1, rr, :DH], gu[1, DH:, :], preferred_element_type=F32)
+        g = jnp.dot(xg[c, rr, :DH], gu[0, own_d, :], preferred_element_type=F32)
+        u = jnp.dot(xg[c, rr, :DH], gu[1, own_d, :], preferred_element_type=F32)
+        for d in groups:
+            others(d)
+        g = g + jnp.dot(xg[1 - c, rr, :DH], gu[0, oth_d, :], preferred_element_type=F32)
+        u = u + jnp.dot(xg[1 - c, rr, :DH], gu[1, oth_d, :], preferred_element_type=F32)
         hid[c, rr, :] = (g / (1.0 + jnp.exp(-g)) * u).astype(BF16)
         h = hid.at[c, rr]
         go(remote(h, h, hs.at[i], hr.at[i], other))
 
-    def down_phase(i, r0):
+    def down_phase(i, r0, groups):
         rr = pl.ds(pl.multiple_of(r0, half), half)
-        h = hid.at[1 - c, rr]
-        remote(h, h, hs.at[i], hr.at[i], other).wait_recv()
         col = lax.broadcasted_iota(jnp.int32, (half, 128), 1)
         wt = xg[0, rr, DH:].astype(F32) + xg[1, rr, DH:].astype(F32)
         wt = jnp.sum(jnp.where(col == me, wt, 0.0), axis=1, keepdims=True)
-        v = jnp.dot(hid[0, rr, :], dw[0], preferred_element_type=F32)
-        v = v + jnp.dot(hid[1, rr, :], dw[1], preferred_element_type=F32)
+        acc[rr, :] = jnp.dot(hid[c, rr, :], dw[c], preferred_element_type=F32)
+        h = hid.at[1 - c, rr]
+        remote(h, h, hs.at[i], hr.at[i], other).wait_recv()
+        v = acc[rr, :] + jnp.dot(hid[1 - c, rr, :], dw[1 - c], preferred_element_type=F32)
         ysend[rr, :] = (v * wt).astype(BF16)
+        for d in groups:
+            send_plane(d)
 
     def slot(j, d):
         return p1.at[pl.ds(((j - 1) * 4 + d) * T, T)]
 
     def send_plane(d):
-        for j in (1, 2, 3):
+        for j in (3, 1, 2):
             go(remote(ysend.at[rows(zd[d], planes[j])], slot(j, d),
                       as_.at[j - 1, d], ar.at[j - 1, d], ex(z, planes[j])))
 
@@ -230,30 +235,26 @@
 
     ra = (z // 2) * half
     rb = half - ra
-    up_phase(0, ra)
+    up_phase(0, ra, (0, 1))
     arrive(2)
     w_d.wait()
     dcopy.wait_recv()
-    down_phase(0, ra)
-    send_plane(1)
-    send_plane(0)
+    down_phase(0, ra, (1, 0))
     arrive(3)
-    others(2)
-    others(3)
-    up_phase(1, rb)
-    down_phase(1, rb)
-    send_plane(3)
-    send_plane(2)
+    up_phase(1, rb, (2, 3))
+    down_phase(1, rb, (3, 2))
     for d in (1, 3, 2):
         p2s[d - 1] = reduce_plane(d).astype(BF16)
         go(remote(p2s.at[d - 1], p2r.at[z], bs.at[d - 1], br.at[z], ex(zd[d], plane)))
     total = reduce_plane(0)
-    for d in (1, 2, 3):
+    for copy in started[:-3]:
+        copy.wait_send()
+    for d in (1, 3, 2):
         s = p2r.at[zd[d]]
         remote(s, s, bs.at[d - 1], br.at[zd[d]], ex(zd[d], plane)).wait_recv()
         total = total + s[...].astype(F32)
     out_ref[...] = total.astype(BF16)
-    for copy in started:
+    for copy in started[-3:]:
         copy.wait_send()
 
 
@@ -275,6 +276,7 @@
             pltpu.VMEM((T, DH), BF16),
             pltpu.VMEM((K, T), jnp.int32),
             pltpu.VMEM((K, T), F32),
+            pltpu.VMEM((R, DH), F32),
             pltpu.VMEM((2, R, DH + 128), BF16),
             pltpu.VMEM((2, D, F), BF16),
             pltpu.VMEM((2, F, DH), BF16),

time: 29.6 us -> 29.2 us (0.986)
  Pallas kernels: 28.1 us -> 27.7 us
    pallas_call x1, Pallas kernels: 28.1 us -> 27.7 us  [fused(): pl.pallas_call(kernel, out_shape=jax.ShapeDtypeStruct((T, DH), BF16), in_...]
where the time goes in v4:
time: 29.2 us; the launch traced here: 29 us
  Pallas kernels  27.7 us (95%)
  local copies, waits for them, and re-layouts  1.38 us (5%)
    pallas_call x1, Pallas kernels, fused(): pl.pallas_call(kernel, out_shape=jax.ShapeDtypeStruct((T, DH), BF16), in_...  27.7 us
    unnamed x1, local copies, waits for them, and re-layouts  1.38 us

profile of v4, /device:TPU:0, one launch (start us, length us, event | category | flops | bytes accessed | tf_op | source)
XLA Modules:
  0.0 29.0 jit_solution(16522653042314118771)
XLA Ops:
  0.0 27.7 %shard_map.64 = bf16[16,1024]{1,0:T(8,128)(2,1)} custom-call(bf16[16,1024]{1,0:T(8,128)(2,1)} %tok_hbm.1, s32[8,16]{1,0:T(8,128)} %bitcast.2, f32[8,16]{1,0:T(8,128)} %bitcast.3, bf16[1,2048,384]{2,1,0:T(8,128)(2,1)} %gate_hbm.1, bf16[1,2048,384]{2,1,0:T(8,128)(2,1)} %up_hbm.1, bf16[1,384,2048]{2,1,0:T(8,128)(2,1)} %down_hbm.1), custom_call_target="tpu_custom_call" | custom-call | flops 1207959552 | bytes 4718592 | tf_op jit(solution)/shard_map/pallas_call | solution.py:270
  27.7 1.4 %copy.8 = bf16[16,1024]{1,0:T(8,128)(2,1)} copy(bf16[16,1024]{1,0:T(8,128)(2,1)} %shard_map.64) | data formatting | bytes 65536

commit v5 on v4

--- a/solution.py
+++ b/solution.py
@@ -159,22 +159,28 @@
             b = block(zd[d], planes[j])
             ss, rs = sems[j]
             remote(b, b, ss.at[d], rs.at[d], ex(z, planes[j])).wait_recv()
-            share(d, j)
+            if d >= 2:
+                share(d, j)
+        if d < 2:
+            b = xg.at[c, rows(zd[d], 0, 4)]
+            go(remote(b, b, ps.at[d, 0], pr.at[d, 0], other))
 
     def zwait(d):
         b = block(zd[d], plane)
         remote(b, b, zs.at[0], zr.at[zd[d]], ex(zd[d], plane)).wait_recv()
 
     def others(d):
+        if d < 2:
+            b = xg.at[1 - c, rows(zd[d], 0, 4)]
+            remote(b, b, ps.at[d, 0], pr.at[d, 0], other).wait_recv()
+            return
         for j in range(4):
             b = block_other(zd[d], planes[j])
             remote(b, b, ps.at[d, j], pr.at[d, j], other).wait_recv()
 
     spread(z, 0, z)
-    share(0, 0)
     zwait(1)
     spread(zd[1], 1, z)
-    share(1, 0)
     arrive(0)
     zwait(2)
     spread(zd[2], 2, z)

time: 29.2 us -> 29.3 us (level)
  no operation moved by 1% of the time
where the time goes in v5:
time: 29.3 us; the launch traced here: 29.1 us
  Pallas kernels  27.8 us (95%)
  local copies, waits for them, and re-layouts  1.38 us (5%)
    pallas_call x1, Pallas kernels, fused(): pl.pallas_call(kernel, out_shape=jax.ShapeDtypeStruct((T, DH), BF16), in_...  27.8 us
    unnamed x1, local copies, waits for them, and re-layouts  1.38 us

profile of v5, /device:TPU:0, one launch (start us, length us, event | category | flops | bytes accessed | tf_op | source)
XLA Modules:
  0.0 29.1 jit_solution(16040836880097525800)
XLA Ops:
  0.0 27.8 %shard_map.64 = bf16[16,1024]{1,0:T(8,128)(2,1)} custom-call(bf16[16,1024]{1,0:T(8,128)(2,1)} %tok_hbm.1, s32[8,16]{1,0:T(8,128)} %bitcast.2, f32[8,16]{1,0:T(8,128)} %bitcast.3, bf16[1,2048,384]{2,1,0:T(8,128)(2,1)} %gate_hbm.1, bf16[1,2048,384]{2,1,0:T(8,128)(2,1)} %up_hbm.1, bf16[1,384,2048]{2,1,0:T(8,128)(2,1)} %down_hbm.1), custom_call_target="tpu_custom_call" | custom-call | flops 1207959552 | bytes 4718592 | tf_op jit(solution)/shard_map/pallas_call | solution.py:276
  27.8 1.4 %copy.8 = bf16[16,1024]{1,0:T(8,128)(2,1)} copy(bf16[16,1024]{1,0:T(8,128)(2,1)} %shard_map.64) | data formatting | bytes 65536
